TPU v7x, 32 devices: a whole 2x2x4 slice. The times are simulated.
32 devices in a mesh: dp: 16 (over z, y, core), seq: 2 (over x).
Axes of the slice: x: 2, y: 2, z: 4, core: 2. Of those that a mesh axis runs over, the one named last changes fastest.
Arguments:
- acts: bfloat16 [4096, 4096], P(('dp', 'seq')), may hold values from -6 to 6
- grad_out: bfloat16 [4096, 4096], P('dp', 'seq'), may hold values from -6 to 6
- proj_weight: bfloat16 [4096, 4096], P('dp', 'seq'), may hold values from -0.09375 to 0.09375
Outputs:
- grad_acts: float32 [4096, 4096], P(('dp', 'seq'))
- grad_weight: float32 [4096, 4096], P('dp', 'seq')
All inputs are finite; a program needn't handle non-finite values.
Results may differ from a plain program's by a relative error of at most 0.014.
Values may be sent and summed in bfloat16 or wider, within the bound.
A program may use at most 128 MiB of HBM per device.

v0:
```python
import jax
import jax.numpy as jnp
from jax import lax
from jax.sharding import PartitionSpec as P


def rounded(value):
    return lax.optimization_barrier(value.astype(jnp.bfloat16)).astype(jnp.float32)


def per_device(acts, grad_out, proj_weight):
    tok_rows = acts.shape[0]
    total_tokens = tok_rows * lax.axis_size("seq") * lax.axis_size("dp")
    full_weight = lax.all_gather(proj_weight, "dp", axis=0, tiled=True)
    whole_term = lax.dot_general(
        grad_out, full_weight, (((1,), (1,)), ((), ())), preferred_element_type=jnp.float32
    )
    summed = lax.psum_scatter(
        whole_term.astype(jnp.bfloat16), "seq", scatter_dimension=0, tiled=True
    ).astype(jnp.float32)
    gathered = lax.all_gather(acts, "seq", axis=0, tiled=True)
    local_term = None
    local_term = rounded(
        lax.dot_general(
            gathered, grad_out, (((0,), (0,)), ((), ())), preferred_element_type=jnp.float32
        )
    )
    wsummed = lax.psum_scatter(local_term, "dp", scatter_dimension=0, tiled=True)
    grad_weight = wsummed / jnp.sqrt(jnp.float32(total_tokens))
    return (summed, grad_weight)


def solution(mesh):
    in_specs = (P(("dp", "seq"), None), P("dp", "seq"), P("dp", "seq"))
    out_specs = (P(("dp", "seq"), None), P("dp", "seq"))
    return jax.shard_map(
        per_device, mesh=mesh, in_specs=in_specs, out_specs=out_specs, check_vma=False
    )
```

profile of v0, /device:TPU:17, one launch (start us, length us, event | category | flops | bytes accessed | tf_op | source)
XLA Modules:
  0.0 551.5 jit_solution(9148058059366858555)
XLA Ops:
  7.2 0.0 copy-start
  7.2 0.0 all-gather.3.cloned.1.call-start
  7.2 0.7 all-gather.3.cloned.1.call-update
  7.9 0.0 all-gather.5.cloned.1.call-start
  8.0 0.7 all-gather.5.cloned.1.call-update
  8.7 0.0 reduce-scatter.3.cloned.1.call-start
  8.7 129.0 %all-gather.3.cloned.1.call-done = bf16[4096,2048]{1,0:T(8,128)(2,1)} async-done(((bf16[256,2048]{1,0:T(8,128)(2,1)}), bf16[4096,2048]{1,0:T(8,128)(2,1)}) %all-gather.3.cloned.1.call-update) | async-done | bytes 16777232 | tf_op jit(solution)/shard_map/all_gather | solution.py:14
  137.7 0.0 copy-done
  137.7 18.0 %convolution_convert_fusion.1 = bf16[256,4096]{1,0:T(8,128)(2,1)} fusion(bf16[256,2048]{1,0:T(8,128)(2,1)S(1)} %copy-done, bf16[4096,2048]{1,0:T(8,128)(2,1)} %all-gather.3.cloned.1.call-done), kind=kOutput, calls=%fused_computation.1 | convolution fusion | flops 4296015872 | bytes 19922944 | tf_op jit(solution)/shard_map/dot_general | solution.py:15
  155.7 0.0 reduce-scatter.3.cloned.1.call-update
  155.7 0.0 reduce-scatter.5.cloned.1.call-start
  155.8 15.3 %all-gather.5.cloned.1.call-done = bf16[256,4096]{1,0:T(8,128)(2,1)} async-done(((bf16[128,4096]{1,0:T(8,128)(2,1)}), bf16[256,4096]{1,0:T(8,128)(2,1)}) %all-gather.5.cloned.1.call-update) | async-done | bytes 2097168 | tf_op jit(solution)/shard_map/all_gather | solution.py:21
  171.0 10.0 %convolution_convert_fusion = bf16[4096,2048]{1,0:T(8,128)(2,1)} fusion(bf16[256,4096]{1,0:T(8,128)(2,1)} %all-gather.5.cloned.1.call-done, bf16[256,2048]{1,0:T(8,128)(2,1)S(1)} %copy-done), kind=kOutput, calls=%fused_computation | convolution fusion | flops 4303355904 | bytes 19922944 | tf_op jit(solution)/shard_map/dot_general | solution.py:24
  181.1 18.7 %convert_element_type.15 = f32[4096,2048]{1,0:T(8,128)} convert(bf16[4096,2048]{1,0:T(8,128)(2,1)} %convolution_convert_fusion) | non-fusion elementwise | flops 8388608 | bytes 50331648 | tf_op jit(solution)/shard_map/convert_element_type | solution.py:8
  199.8 0.0 reduce-scatter.5.cloned.1.call-update
  199.8 5.9 %reduce-scatter.3.cloned.1.call-done = bf16[128,4096]{1,0:T(8,128)(2,1)} async-done(((bf16[256,4096]{1,0:T(8,128)(2,1)}), bf16[128,4096]{1,0:T(8,128)(2,1)}) %reduce-scatter.3.cloned.1.call-update) | async-done | bytes 1048592 | tf_op jit(solution)/shard_map/reduce_scatter | solution.py:18
  205.7 0.0 copy-start.1
  205.7 2.8 convert_element_type.13
  208.6 333.2 %reduce-scatter.5.cloned.1.call-done = f32[256,2048]{1,0:T(8,128)} async-done(((f32[4096,2048]{1,0:T(8,128)}), f32[256,2048]{1,0:T(8,128)}) %reduce-scatter.5.cloned.1.call-update) | async-done | bytes 2097168 | tf_op jit(solution)/shard_map/reduce_scatter | solution.py:28
  541.8 3.1 broadcast_multiply_fusion
  544.9 0.0 copy-done.1
Async XLA Ops:
  7.2 130.5 %copy-start = (bf16[256,2048]{1,0:T(8,128)(2,1)S(1)}, bf16[256,2048]{1,0:T(8,128)(2,1)}, u32[]{:S(2)}) copy-start(bf16[256,2048]{1,0:T(8,128)(2,1)} %param.4) | copy-start | bytes 3145732
  7.2 130.5 %all-gather.3.cloned.1.call-start = ((), (), s32[]{:S(2)}) async-start(), calls=%async_computation.2 | async-start | bytes 17825792 | tf_op jit(solution)/shard_map/all_gather | solution.py:14
  7.9 163.1 %all-gather.5.cloned.1.call-start = ((), (), s32[]{:S(2)}) async-start(), calls=%async_computation.4 | async-start | bytes 3145728 | tf_op jit(solution)/shard_map/all_gather | solution.py:21
  8.7 197.0 %reduce-scatter.3.cloned.1.call-start = ((), (), s32[]{:S(2)}) async-start(), calls=%async_computation.3 | async-start | bytes 3145728 | tf_op jit(solution)/shard_map/reduce_scatter | solution.py:18
  155.7 386.1 %reduce-scatter.5.cloned.1.call-start = ((), (), s32[]{:S(2)}) async-start(), calls=%async_computation.5 | async-start | bytes 35651584 | tf_op jit(solution)/shard_map/reduce_scatter | solution.py:28
  205.7 339.2 %copy-start.1 = (bf16[256,2048]{1,0:T(8,128)(2,1)S(1)}, bf16[256,2048]{1,0:T(8,128)(2,1)}, u32[]{:S(2)}) copy-start(bf16[256,2048]{1,0:T(8,128)(2,1)} %param.4) | copy-start | bytes 3145732
Sparse Core Ops, SparseCore 0:
  10.2 127.4 all-gather.2
  139.2 31.7 all-gather.4
  173.9 31.8 reduce-scatter.2
  210.4 331.3 reduce-scatter.4
where the time goes:
time: 555 us; the launch traced here: 551 us
  waiting for transfers between devices  485 us (87%)
  matrix products  28 us (5%)
  other arithmetic  24.7 us (4%)
  between operations  13.8 us (2%)
    reduce_scatter x1, waiting for transfers between devices, per_device(): lax.psum_scatter(local_term, 'dp', scatter_dimension=0, tiled=True)  333 us
    all_gather x1, waiting for transfers between devices, per_device(): full_weight = lax.all_gather(proj_weight, 'dp', axis=0, tiled=True)  129 us
    convert_element_type x1, other arithmetic, rounded(): lax.optimization_barrier(value.astype(jnp.bfloat16)).astype(jnp.float32)  18.7 us
    dot_general x1, matrix products, per_device(): lax.dot_general(grad_out, full_weight, (((1,), (1,)), ((), ())), preferre...  18 us
    all_gather x1, waiting for transfers between devices, per_device(): gathered = lax.all_gather(acts, 'seq', axis=0, tiled=True)  15.3 us
  transfers between devices with their start and end apart: 4, of which 4 were waited for; matrix products, arithmetic and copies ran while one was open for 9% of the time, Pallas kernels for 0%

commit v1 on v0

v1 whole, which is shorter than its diff:
```python
import functools

import jax
import jax.numpy as jnp
from jax import lax
from jax.experimental import pallas as pl
from jax.experimental.pallas import tpu as pltpu
from jax.sharding import PartitionSpec as P

MESH = pl.DeviceIdType.MESH
NQ = 4
PIECES = 2
BF16 = jnp.bfloat16
F32 = jnp.float32


def kernel(nz, ns, acts, go, w, ga_out, rs_out, pz_out, go_l, acts_l, wall, ga_s,
           acts_t, rr, sb, pbuf, go_send, go_recv, a_send, a_recv, ga_send, ga_recv,
           z_send, z_recv, l_sem):
    tok = acts.shape[0]
    rg, cols = go.shape
    blk = w.shape[0]
    h = blk // PIECES
    total = NQ * rg
    dp = lax.axis_index("dp")
    x = lax.axis_index("seq")
    z = dp // NQ
    q = dp % NQ
    mirror = nz - 1 - z
    pos = (z, mirror)

    def real(d, i):
        return i if d == 0 else nz - 1 - i

    def layer(qq, xx):
        return {"dp": z * NQ + qq, "seq": xx}

    def ahead(d):
        return {"dp": (z + (1 if d == 0 else -1)) * NQ + q, "seq": x}

    def part(i, size):
        return pl.ds(pl.multiple_of(i * size, size), size)

    barrier = pltpu.get_barrier_semaphore()
    for o in range(NQ * ns):
        @pl.when(o != q * ns + x)
        def _():
            pl.semaphore_signal(barrier, inc=1, device_id=layer(o // ns, o % ns), device_id_type=MESH)
    for d in range(2):
        @pl.when(pos[d] < nz - 1)
        def _():
            pl.semaphore_signal(barrier, inc=1, device_id=ahead(d), device_id_type=MESH)
    beside = (z + nz - 1) // nz + (mirror + nz - 1) // nz
    pl.semaphore_wait(barrier, NQ * ns - 1 + beside)

    def zcopy(d, t, s, src, dst):
        return pltpu.make_async_remote_copy(
            src_ref=src, dst_ref=dst, send_sem=z_send.at[d, t, s], recv_sem=z_recv.at[d, t, s],
            device_id=ahead(d), device_id_type=MESH)

    def wall_piece(i, s):
        return wall.at[pl.ds(pl.multiple_of(i * blk + s * h, h), h)]

    def rows(s):
        return pl.ds(s * h, h)

    for s in range(PIECES):
        for d in range(2):
            @pl.when(pos[d] < nz - 1)
            def _():
                zcopy(d, 0, s, w.at[rows(s)], wall_piece(z, s)).start()

    sib = q + 1 - 2 * (q % 2)
    far = (q + 2) % NQ
    sibfar = (sib + 2) % NQ

    def gcopy(k, src, slot, target):
        return pltpu.make_async_remote_copy(
            src_ref=src, dst_ref=go_l.at[part(slot, rg)], send_sem=go_send.at[k],
            recv_sem=go_recv.at[k], device_id=layer(target, x), device_id_type=MESH)

    gcopy(1, go, q, far).start()
    gcopy(0, go, q, sib).start()
    own_go = pltpu.make_async_copy(go, go_l.at[part(q, rg)], l_sem.at[0])
    own_go.start()
    own_w = pltpu.make_async_copy(w, wall.at[part(z, blk)], l_sem.at[1])
    own_w.start()
    gcopy(1, go, far, far).wait_recv()
    gcopy(2, go_l.at[part(far, rg)], far, sib).start()

    def send_acts(m):
        for o in range(NQ * ns):
            qq, xx = o // ns, o % ns
            src = acts.at[:, part(m * NQ + qq, blk)]
            dst = acts_l.at[part(q * ns + x, tok), part(m, blk)]

            @pl.when(o == q * ns + x)
            def _():
                pltpu.make_async_copy(src, dst, a_recv.at[m]).start()

            @pl.when(o != q * ns + x)
            def _():
                pltpu.make_async_remote_copy(
                    src_ref=src, dst_ref=dst, send_sem=a_send, recv_sem=a_recv.at[m],
                    device_id=layer(qq, xx), device_id_type=MESH).start()

    for t in range(1, nz):
        for d in range(2):
            @pl.when(t > pos[d])
            def _():
                send_acts(real(d, nz - t + pos[d]))
    send_acts(z)

    gcopy(0, go, sib, sib).wait_recv()
    gcopy(2, go, sibfar, sib).wait_recv()
    own_go.wait()
    own_w.wait()

    def input_grad(m):
        @pl.loop(0, NQ)
        def _(qq):
            out = lax.dot_general(
                go_l[part(qq, rg), :], wall[part(m, blk), :], (((1,), (1,)), ((), ())),
                preferred_element_type=F32)
            ga_s[part(qq, rg), part(m, blk)] = out.astype(BF16)
            for xx in range(ns):
                src = ga_s.at[part(qq * ns + xx, tok), part(m, blk)]
                dst = ga_out.at[x, :, part(m * NQ + q, blk)]
                mine = (qq * ns + xx) == (q * ns + x)

                @pl.when(mine)
                def _():
                    pltpu.make_async_copy(src, dst, ga_recv).start()

                @pl.when(jnp.logical_not(mine))
                def _():
                    pltpu.make_async_remote_copy(
                        src_ref=src, dst_ref=dst, send_sem=ga_send, recv_sem=ga_recv,
                        device_id=layer(qq, xx), device_id_type=MESH).start()

    tile = min(cols, 512)

    def weight_grad(m, slot):
        block = acts_l.at[:, part(m, blk)]
        pltpu.make_async_copy(block, block, a_recv.at[m]).wait()
        acts_t[...] = acts_l[:, part(m, blk)].T

        @pl.loop(0, cols // tile)
        def _(j):
            pbuf[slot, :, part(j, tile)] = jnp.dot(
                acts_t[...], go_l[:, part(j, tile)], preferred_element_type=F32)

    step = min(h, 32)

    def forward_sum(d, t, s):
        def emit(add):
            @pl.loop(0, h // step)
            def _(i):
                r = pl.ds(pl.multiple_of(s * h + i * step, step), step)
                value = pbuf[d, r, :]
                if add:
                    value = value + rr[d, t - 1, r, :].astype(F32)
                sb[d, t - 1, r, :] = value.astype(BF16)

        @pl.when(pos[d] > 0)
        def _():
            piece = rr.at[d, t - 1, rows(s)]
            zcopy(d, t - 1, s, piece, piece).wait_recv()
            emit(True)

        @pl.when(pos[d] == 0)
        def _():
            emit(False)

        dst = rs_out.at[d, rows(s)] if t == nz - 1 else rr.at[d, t, rows(s)]
        zcopy(d, t, s, sb.at[d, t - 1, rows(s)], dst).start()

    def pass_weight(d, t, s):
        piece = wall_piece(real(d, pos[d] - t), s)
        zcopy(d, t - 1, s, piece, piece).wait_recv()

        @pl.when(pos[d] < nz - 1)
        def _():
            zcopy(d, t, s, piece, piece).start()

    input_grad(z)
    for t in range(1, nz):
        for d in range(2):
            @pl.when(t > pos[d])
            def _():
                weight_grad(real(d, nz - t + pos[d]), d)
        for s in range(PIECES):
            for d in range(2):
                @pl.when(t <= pos[d])
                def _():
                    pass_weight(d, t, s)

                @pl.when(t > pos[d])
                def _():
                    forward_sum(d, t, s)
        for d in range(2):
            @pl.when(t <= pos[d])
            def _():
                input_grad(real(d, pos[d] - t))

    weight_grad(z, 2)
    own_p = pltpu.make_async_copy(pbuf.at[2], pz_out, l_sem.at[0])
    own_p.start()
    for d in range(2):
        @pl.when(pos[d] == 0)
        def _():
            rr[d, 0] = jnp.zeros((blk, cols), BF16)
            fill = pltpu.make_async_copy(rr.at[d, 0], rs_out.at[d], l_sem.at[1])
            fill.start()
            fill.wait()

        @pl.when(pos[d] > 0)
        def _():
            for s in range(PIECES):
                piece = rs_out.at[d, rows(s)]
                zcopy(d, nz - 1, s, piece, piece).wait_recv()

    pltpu.make_async_copy(ga_out, ga_out, ga_recv).wait()
    own_p.wait()
    for d in range(2):
        @pl.when(pos[d] < nz - 1)
        def _():
            for t in range(nz):
                for s in range(PIECES):
                    piece = sb.at[d, 0, rows(s)]
                    zcopy(d, t, s, piece, piece).wait_send()
    for k in range(3):
        gcopy(k, go, q, sib).wait_send()
    others = acts_l.at[pl.ds(0, total - tok)]
    pltpu.make_async_copy(others, others, a_send).wait()
    others = ga_s.at[pl.ds(0, total - tok)]
    pltpu.make_async_copy(others, others, ga_send).wait()


def per_device(acts, grad_out, proj_weight):
    ns = lax.axis_size("seq")
    nz = lax.axis_size("dp") // NQ
    tok, feats = acts.shape
    rg, cols = grad_out.shape
    blk = proj_weight.shape[0]
    total_tokens = tok * ns * nz * NQ
    total = NQ * rg
    anywhere = pl.BlockSpec(memory_space=pl.ANY)
    flops = 4 * total * nz * blk * cols
    parts, sums, own = pl.pallas_call(
        functools.partial(kernel, nz, ns),
        out_shape=(
            jax.ShapeDtypeStruct((ns, tok, feats), BF16),
            jax.ShapeDtypeStruct((2, blk, cols), BF16),
            jax.ShapeDtypeStruct((blk, cols), F32),
        ),
        in_specs=[anywhere] * 3,
        out_specs=(anywhere,) * 3,
        scratch_shapes=[
            pltpu.VMEM((total, cols), BF16),
            pltpu.VMEM((total, nz * blk), BF16),
            pltpu.VMEM((nz * blk, cols), BF16),
            pltpu.VMEM((total, nz * blk), BF16),
            pltpu.VMEM((blk, total), BF16),
            pltpu.VMEM((2, nz - 1, blk, cols), BF16),
            pltpu.VMEM((2, nz - 1, blk, cols), BF16),
            pltpu.VMEM((3, blk, cols), F32),
            pltpu.SemaphoreType.DMA((3,)),
            pltpu.SemaphoreType.DMA((3,)),
            pltpu.SemaphoreType.DMA,
            pltpu.SemaphoreType.DMA((nz,)),
            pltpu.SemaphoreType.DMA,
            pltpu.SemaphoreType.DMA,
            pltpu.SemaphoreType.DMA((2, nz, PIECES)),
            pltpu.SemaphoreType.DMA((2, nz, PIECES)),
            pltpu.SemaphoreType.DMA((2,)),
        ],
        compiler_params=pltpu.CompilerParams(
            collective_id=0, has_side_effects=True, vmem_limit_bytes=48 * 1024 * 1024),
        cost_estimate=pl.CostEstimate(flops=flops, bytes_accessed=16 * 1024 * 1024, transcendentals=0),
    )(acts, grad_out, proj_weight)
    grad_acts = jnp.sum(parts.astype(F32), axis=0)
    summed = own + sums[0].astype(F32) + sums[1].astype(F32)
    grad_weight = summed / jnp.sqrt(jnp.float32(total_tokens))
    return (grad_acts, grad_weight)


def solution(mesh):
    in_specs = (P(("dp", "seq"), None), P("dp", "seq"), P("dp", "seq"))
    out_specs = (P(("dp", "seq"), None), P("dp", "seq"))
    return jax.shard_map(
        per_device, mesh=mesh, in_specs=in_specs, out_specs=out_specs, check_vma=False
    )
```

time: 555 us -> 115 us (0.21)
  waiting for transfers between devices: 485 us -> 0 us
  Pallas kernels: 0 us -> 106 us
  matrix products: 28 us -> 0 us
  other arithmetic: 24.7 us -> 3.47 us
  between operations: 13.8 us -> 0.67 us
    reduce_scatter x2 -> x0, waiting for transfers between devices: 339 us -> none  [the longest x1 333 us: per_device(): lax.psum_scatter(local_term, 'dp', scatter_dimension=0, tiled=True)]
    all_gather x2 -> x0, waiting for transfers between devices: 144 us -> none  [the longest x1 129 us: per_device(): full_weight = lax.all_gather(proj_weight, 'dp', axis=0, tiled=True)]
    pallas_call x0 -> x1, Pallas kernels: none -> 106 us  [per_device(): pl.pallas_call(functools.partial(kernel, nz, ns), out_shape=(jax.ShapeDty...]
    dot_general x2 -> x0, matrix products: 28 us -> none  [the longest x1 18 us: per_device(): lax.dot_general(grad_out, full_weight, (((1,), (1,)), ((), ())), preferre...]
    convert_element_type x2 -> x0, other arithmetic: 21.6 us -> none  [the longest x1 18.7 us: rounded(): lax.optimization_barrier(value.astype(jnp.bfloat16)).astype(jnp.float32)]
  transfers between devices with their start and end apart: 4 -> 0, of which waited for: 4 -> 0; matrix products, arithmetic and copies ran while one was open for 9% -> 0% of each run, Pallas kernels for 0% -> 0%
where the time goes in v1:
time: 115 us
  Pallas kernels  106 us (92%)
  local copies, waits for them, and re-layouts  4.93 us (4%)
  other arithmetic  3.47 us (3%)
    pallas_call x1, Pallas kernels, per_device(): pl.pallas_call(functools.partial(kernel, nz, ns), out_shape=(jax.ShapeDty...  106 us
    unnamed x10, local copies, waits for them, and re-layouts  4.93 us

profile of v1, /device:TPU:17, one launch (start us, length us, event | category | flops | bytes accessed | tf_op | source)
XLA Modules:
  0.0 114.9 jit_solution(6911207406361979210)
XLA Ops:
  0.6 0.0 copy-start
  0.6 1.2 %copy-done = bf16[128,4096]{1,0:T(8,128)(2,1)S(1)} copy-done((bf16[128,4096]{1,0:T(8,128)(2,1)S(1)}, bf16[128,4096]{1,0:T(8,128)(2,1)}, u32[]{:S(2)}) %copy-start) | copy-done | bytes 1048600
  1.9 0.0 copy-start.1
  1.9 1.2 %copy-done.1 = bf16[256,2048]{1,0:T(8,128)(2,1)S(1)} copy-done((bf16[256,2048]{1,0:T(8,128)(2,1)S(1)}, bf16[256,2048]{1,0:T(8,128)(2,1)}, u32[]{:S(2)}) %copy-start.1) | copy-done | bytes 1048600
  3.1 0.0 copy-start.2
  3.1 1.2 %copy-done.2 = bf16[256,2048]{1,0:T(8,128)(2,1)S(1)} copy-done((bf16[256,2048]{1,0:T(8,128)(2,1)S(1)}, bf16[256,2048]{1,0:T(8,128)(2,1)}, u32[]{:S(2)}) %copy-start.2) | copy-done | bytes 1048600
  4.3 105.9 %shard_map.50 = (bf16[2,128,4096]{2,1,0:T(8,128)(2,1)S(1)}, bf16[2,256,2048]{2,1,0:T(8,128)(2,1)}, f32[256,2048]{1,0:T(8,128)}) custom-call(bf16[128,4096]{1,0:T(8,128)(2,1)S(1)} %copy-done, bf16[256,2048]{1,0:T(8,128)(2,1)S(1)} %copy-done.1, bf16[256,2048]{1,0:T(8,128)(2,1)S(1)} %copy-done.2), custom_call_target="tpu_custom_call" | custom-call | flops 8589934592 | bytes 16777216 | tf_op jit(solution)/shard_map/pallas_call | solution.py:250
  110.2 0.0 copy-start.3
  110.2 0.0 copy-start.4
  110.2 1.7 %convert_reduce_fusion = f32[128,4096]{1,0:T(8,128)} fusion(bf16[2,128,4096]{2,1,0:T(8,128)(2,1)S(1)} %get-tuple-element.5), kind=kLoop, calls=%fused_computation | loop fusion | flops 1572864 | bytes 4194304 | tf_op jit(solution)/shard_map/reduce_sum | solution.py:282
  111.9 0.4 copy-done.3
  112.3 0.9 copy-done.4
  113.2 1.8 %fusion = f32[256,2048]{1,0:T(8,128)} fusion(f32[256,2048]{1,0:T(8,128)S(1)} %copy-done.4, bf16[2,256,2048]{2,1,0:T(8,128)(2,1)S(1)} %copy-done.3), kind=kLoop, calls=%fused_computation.2 | loop fusion | flops 2621440 | bytes 6291456 | tf_op jit(solution)/shard_map/div | solution.py:284
Async XLA Ops:
  0.6 1.2 %copy-start = (bf16[128,4096]{1,0:T(8,128)(2,1)S(1)}, bf16[128,4096]{1,0:T(8,128)(2,1)}, u32[]{:S(2)}) copy-start(bf16[128,4096]{1,0:T(8,128)(2,1)} %acts.1) | copy-start | bytes 3145732
  1.9 1.2 %copy-start.1 = (bf16[256,2048]{1,0:T(8,128)(2,1)S(1)}, bf16[256,2048]{1,0:T(8,128)(2,1)}, u32[]{:S(2)}) copy-start(bf16[256,2048]{1,0:T(8,128)(2,1)} %go.1) | copy-start | bytes 3145732
  3.1 1.2 %copy-start.2 = (bf16[256,2048]{1,0:T(8,128)(2,1)S(1)}, bf16[256,2048]{1,0:T(8,128)(2,1)}, u32[]{:S(2)}) copy-start(bf16[256,2048]{1,0:T(8,128)(2,1)} %w.1) | copy-start | bytes 3145732
  110.2 2.1 %copy-start.3 = (bf16[2,256,2048]{2,1,0:T(8,128)(2,1)S(1)}, bf16[2,256,2048]{2,1,0:T(8,128)(2,1)}, u32[]{:S(2)}) copy-start(bf16[2,256,2048]{2,1,0:T(8,128)(2,1)} %get-tuple-element.7) | copy-start | bytes 6291460
  110.2 3.0 %copy-start.4 = (f32[256,2048]{1,0:T(8,128)S(1)}, f32[256,2048]{1,0:T(8,128)}, u32[]{:S(2)}) copy-start(f32[256,2048]{1,0:T(8,128)} %get-tuple-element.6) | copy-start | bytes 6291460

commit v2 on v1

v2 whole, which is shorter than its diff:
```python
import functools

import jax
import jax.numpy as jnp
from jax import lax
from jax.experimental import pallas as pl
from jax.experimental.pallas import tpu as pltpu
from jax.sharding import PartitionSpec as P

MESH = pl.DeviceIdType.MESH
NQ = 4
PIECES = 4
BF16 = jnp.bfloat16
F32 = jnp.float32


def kernel(nz, ns, acts, go, w, ga_out, rs_out, pz_out, go_l, acts_l, wall, ga_s,
           acts_t, rr, sb, pbuf, own, go_send, go_recv, a_send, a_recv, ga_send, ga_recv,
           z_send, z_recv, l_sem):
    tok = acts.shape[0]
    rg, cols = go.shape
    blk = w.shape[0]
    h = blk // PIECES
    pw = cols // PIECES
    total = NQ * rg
    dp = lax.axis_index("dp")
    x = lax.axis_index("seq")
    z = dp // NQ
    q = dp % NQ
    mirror = nz - 1 - z
    pos = (z, mirror)

    def real(d, i):
        return i if d == 0 else nz - 1 - i

    def layer(qq, xx):
        return {"dp": z * NQ + qq, "seq": xx}

    def ahead(d):
        return {"dp": (z + (1 if d == 0 else -1)) * NQ + q, "seq": x}

    def part(i, size):
        return pl.ds(pl.multiple_of(i * size, size), size)

    barrier = pltpu.get_barrier_semaphore()
    for o in range(NQ * ns):
        @pl.when(o != q * ns + x)
        def _():
            pl.semaphore_signal(barrier, inc=1, device_id=layer(o // ns, o % ns), device_id_type=MESH)
    for d in range(2):
        @pl.when(pos[d] < nz - 1)
        def _():
            pl.semaphore_signal(barrier, inc=1, device_id=ahead(d), device_id_type=MESH)
    beside = (z + nz - 1) // nz + (mirror + nz - 1) // nz
    pl.semaphore_wait(barrier, NQ * ns - 1 + beside)

    def zcopy(d, t, s, src, dst):
        return pltpu.make_async_remote_copy(
            src_ref=src, dst_ref=dst, send_sem=z_send.at[d, t, s], recv_sem=z_recv.at[d, t, s],
            device_id=ahead(d), device_id_type=MESH)

    def wall_piece(i, s):
        return wall.at[pl.ds(pl.multiple_of(i * blk + s * h, h), h)]

    for s in range(PIECES):
        for d in range(2):
            @pl.when(pos[d] < nz - 1)
            def _():
                zcopy(d, 0, s, w.at[part(s, h)], wall_piece(z, s)).start()

    sib = q + 1 - 2 * (q % 2)
    far = (q + 2) % NQ
    sibfar = (sib + 2) % NQ

    def gcopy(k, s, slot, target):
        src = go.at[:, part(s, pw)] if k < 2 else go_l.at[part(slot, rg), part(s, pw)]
        return pltpu.make_async_remote_copy(
            src_ref=src, dst_ref=go_l.at[part(slot, rg), part(s, pw)], send_sem=go_send.at[k, s],
            recv_sem=go_recv.at[k, s], device_id=layer(target, x), device_id_type=MESH)

    def send_acts(m):
        @pl.loop(0, NQ * ns)
        def _(o):
            qq, xx = o // ns, o % ns
            src = acts.at[:, part(m * NQ + qq, blk)]
            dst = acts_l.at[part(q * ns + x, tok), part(m, blk)]

            @pl.when(o == q * ns + x)
            def _():
                pltpu.make_async_copy(src, dst, a_recv.at[m]).start()

            @pl.when(o != q * ns + x)
            def _():
                pltpu.make_async_remote_copy(
                    src_ref=src, dst_ref=dst, send_sem=a_send, recv_sem=a_recv.at[m],
                    device_id=layer(qq, xx), device_id_type=MESH).start()

    def send_acts_for(t):
        for d in range(2):
            @pl.when(t > pos[d])
            def _():
                send_acts(real(d, nz - t + pos[d]))

    gcopy(1, 0, q, far).start()
    gcopy(0, 0, q, sib).start()
    send_acts_for(1)
    own_go = pltpu.make_async_copy(go, go_l.at[part(q, rg)], l_sem.at[0])
    own_go.start()
    own_w = pltpu.make_async_copy(w, wall.at[part(z, blk)], l_sem.at[1])
    own_w.start()

    def gather_piece(s):
        gcopy(1, s, far, far).wait_recv()

        @pl.when(s + 1 < PIECES)
        def _():
            gcopy(1, s + 1, q, far).start()
            gcopy(0, s + 1, q, sib).start()

        gcopy(2, s, far, sib).start()

        @pl.when(s == PIECES - 1)
        def _():
            for t in range(2, nz):
                send_acts_for(t)
            send_acts(z)

        gcopy(0, s, sib, sib).wait_recv()
        gcopy(2, s, sibfar, sib).wait_recv()

        @pl.when(s == 0)
        def _():
            own_go.wait()
            own_w.wait()

    def input_grad(m):
        @pl.loop(0, NQ)
        def _(qq):
            out = lax.dot_general(
                go_l[part(qq, rg), :], wall[part(m, blk), :], (((1,), (1,)), ((), ())),
                preferred_element_type=F32)
            ga_s[part(qq, rg), part(m, blk)] = out.astype(BF16)

            @pl.loop(0, ns)
            def _(xx):
                src = ga_s.at[part(qq * ns + xx, tok), part(m, blk)]
                dst = ga_out.at[x, :, part(m * NQ + q, blk)]
                mine = (qq * ns + xx) == (q * ns + x)

                @pl.when(mine)
                def _():
                    pltpu.make_async_copy(src, dst, ga_recv).start()

                @pl.when(jnp.logical_not(mine))
                def _():
                    pltpu.make_async_remote_copy(
                        src_ref=src, dst_ref=dst, send_sem=ga_send, recv_sem=ga_recv,
                        device_id=layer(qq, xx), device_id_type=MESH).start()

    def turn_acts(m, slot):
        block = acts_l.at[:, part(m, blk)]
        pltpu.make_async_copy(block, block, a_recv.at[m]).wait()
        acts_t[slot] = acts_l[:, part(m, blk)].T

    def weight_piece(slot, s):
        return jnp.dot(acts_t[slot], go_l[:, part(s, pw)], preferred_element_type=F32)

    step = min(blk, 64)

    def forward_sum(d, t, s):
        pbuf[d] = weight_piece(d, s)

        def emit(add):
            @pl.loop(0, blk // step)
            def _(i):
                r = part(i, step)
                value = pbuf[d, r, :]
                if add:
                    value = value + rr[d, t - 1, s, r, :].astype(F32)
                sb[d, t - 1, s, r, :] = value.astype(BF16)

        @pl.when(pos[d] > 0)
        def _():
            piece = rr.at[d, t - 1, s]
            zcopy(d, t - 1, s, piece, piece).wait_recv()
            emit(True)

        @pl.when(pos[d] == 0)
        def _():
            emit(False)

        dst = rs_out.at[d, :, part(s, pw)] if t == nz - 1 else rr.at[d, t, s]
        zcopy(d, t, s, sb.at[d, t - 1, s], dst).start()

    def pass_weight(d, t, s):
        piece = wall_piece(real(d, pos[d] - t), s)
        zcopy(d, t - 1, s, piece, piece).wait_recv()

        @pl.when(pos[d] < nz - 1)
        def _():
            zcopy(d, t, s, piece, piece).start()

    for t in range(1, nz):
        @pl.loop(0, PIECES)
        def _(s):
            if t == 1:
                gather_piece(s)

            @pl.when(s == 0)
            def _():
                for d in range(2):
                    @pl.when(t > pos[d])
                    def _():
                        turn_acts(real(d, nz - t + pos[d]), d)

            for d in range(2):
                @pl.when(t <= pos[d])
                def _():
                    pass_weight(d, t, s)

                @pl.when(t > pos[d])
                def _():
                    forward_sum(d, t, s)

            if t == 1:
                @pl.when(s == PIECES - 1)
                def _():
                    input_grad(z)
            else:
                for d in range(2):
                    @pl.when((s == d) & (t - 1 <= pos[d]))
                    def _():
                        input_grad(real(d, pos[d] - (t - 1)))

    for d in range(2):
        @pl.when(nz - 1 <= pos[d])
        def _():
            input_grad(real(d, pos[d] - (nz - 1)))

    turn_acts(z, 0)

    @pl.loop(0, PIECES)
    def _(s):
        own[:, part(s, pw)] = weight_piece(0, s)

    own_p = pltpu.make_async_copy(own, pz_out, l_sem.at[0])
    own_p.start()
    for d in range(2):
        @pl.when(pos[d] == 0)
        def _():
            rr[d, 0] = jnp.zeros((PIECES, blk, pw), BF16)
            for s in range(PIECES):
                fill = pltpu.make_async_copy(rr.at[d, 0, s], rs_out.at[d, :, part(s, pw)], l_sem.at[1])
                fill.start()
                fill.wait()

        @pl.when(pos[d] > 0)
        def _():
            for s in range(PIECES):
                piece = rs_out.at[d, :, part(s, pw)]
                zcopy(d, nz - 1, s, piece, piece).wait_recv()

    pltpu.make_async_copy(ga_out, ga_out, ga_recv).wait()
    own_p.wait()
    for d in range(2):
        @pl.when(pos[d] < nz - 1)
        def _():
            for t in range(nz):
                @pl.loop(0, PIECES)
                def _(s):
                    piece = sb.at[d, 0, s]
                    zcopy(d, t, s, piece, piece).wait_send()
    for k in range(3):
        @pl.loop(0, PIECES)
        def _(s):
            gcopy(k, s, q, sib).wait_send()
    others = acts_l.at[pl.ds(0, total - tok)]
    pltpu.make_async_copy(others, others, a_send).wait()
    others = ga_s.at[pl.ds(0, total - tok)]
    pltpu.make_async_copy(others, others, ga_send).wait()


def per_device(acts, grad_out, proj_weight):
    ns = lax.axis_size("seq")
    nz = lax.axis_size("dp") // NQ
    tok, feats = acts.shape
    rg, cols = grad_out.shape
    blk = proj_weight.shape[0]
    total_tokens = tok * ns * nz * NQ
    total = NQ * rg
    anywhere = pl.BlockSpec(memory_space=pl.ANY)
    flops = 4 * total * nz * blk * cols
    parts, sums, own = pl.pallas_call(
        functools.partial(kernel, nz, ns),
        out_shape=(
            jax.ShapeDtypeStruct((ns, tok, feats), BF16),
            jax.ShapeDtypeStruct((2, blk, cols), BF16),
            jax.ShapeDtypeStruct((blk, cols), F32),
        ),
        in_specs=[anywhere] * 3,
        out_specs=(anywhere,) * 3,
        scratch_shapes=[
            pltpu.VMEM((total, cols), BF16),
            pltpu.VMEM((total, nz * blk), BF16),
            pltpu.VMEM((nz * blk, cols), BF16),
            pltpu.VMEM((total, nz * blk), BF16),
            pltpu.VMEM((2, blk, total), BF16),
            pltpu.VMEM((2, nz - 1, PIECES, blk, cols // PIECES), BF16),
            pltpu.VMEM((2, nz - 1, PIECES, blk, cols // PIECES), BF16),
            pltpu.VMEM((2, blk, cols // PIECES), F32),
            pltpu.VMEM((blk, cols), F32),
            pltpu.SemaphoreType.DMA((3, PIECES)),
            pltpu.SemaphoreType.DMA((3, PIECES)),
            pltpu.SemaphoreType.DMA,
            pltpu.SemaphoreType.DMA((nz,)),
            pltpu.SemaphoreType.DMA,
            pltpu.SemaphoreType.DMA,
            pltpu.SemaphoreType.DMA((2, nz, PIECES)),
            pltpu.SemaphoreType.DMA((2, nz, PIECES)),
            pltpu.SemaphoreType.DMA((2,)),
        ],
        compiler_params=pltpu.CompilerParams(
            collective_id=0, has_side_effects=True, vmem_limit_bytes=62 * 1024 * 1024),
        cost_estimate=pl.CostEstimate(flops=flops, bytes_accessed=16 * 1024 * 1024, transcendentals=0),
    )(acts, grad_out, proj_weight)
    grad_acts = jnp.sum(parts.astype(F32), axis=0)
    summed = own + sums[0].astype(F32) + sums[1].astype(F32)
    grad_weight = summed / jnp.sqrt(jnp.float32(total_tokens))
    return (grad_acts, grad_weight)


def solution(mesh):
    in_specs = (P(("dp", "seq"), None), P("dp", "seq"), P("dp", "seq"))
    out_specs = (P(("dp", "seq"), None), P("dp", "seq"))
    return jax.shard_map(
        per_device, mesh=mesh, in_specs=in_specs, out_specs=out_specs, check_vma=False
    )
```

time: 115 us -> 104 us (0.904); the launches traced: 115 us -> 103 us
  Pallas kernels: 106 us -> 96.6 us
  local copies, waits for them, and re-layouts: 4.93 us -> 0.01 us
  other arithmetic: 3.47 us -> 5.42 us
    pallas_call x1, Pallas kernels: 106 us -> 96.6 us  [per_device(): pl.pallas_call(functools.partial(kernel, nz, ns), out_shape=(jax.ShapeDty...]
    unnamed x10 -> x4, local copies, waits for them, and re-layouts: 4.93 us -> 0.01 us
    reduce_sum x1, other arithmetic: 1.7 us -> 3.65 us  [per_device(): grad_acts = jnp.sum(parts.astype(F32), axis=0)]
where the time goes in v2:
time: 104 us; the launch traced here: 103 us
  Pallas kernels  96.6 us (93%)
  other arithmetic  5.42 us (5%)
    pallas_call x1, Pallas kernels, per_device(): pl.pallas_call(functools.partial(kernel, nz, ns), out_shape=(jax.ShapeDty...  96.6 us
    reduce_sum x1, other arithmetic, per_device(): grad_acts = jnp.sum(parts.astype(F32), axis=0)  3.65 us

profile of v2, /device:TPU:17, one launch (start us, length us, event | category | flops | bytes accessed | tf_op | source)
XLA Modules:
  0.0 102.7 jit_solution(3802371627996946695)
XLA Ops:
  0.6 96.6 %shard_map.50 = (bf16[2,128,4096]{2,1,0:T(8,128)(2,1)}, bf16[2,256,2048]{2,1,0:T(8,128)(2,1)}, f32[256,2048]{1,0:T(8,128)}) custom-call(bf16[128,4096]{1,0:T(8,128)(2,1)} %acts.1, bf16[256,2048]{1,0:T(8,128)(2,1)} %go.1, bf16[256,2048]{1,0:T(8,128)(2,1)} %w.1), custom_call_target="tpu_custom_call" | custom-call | flops 8589934592 | bytes 16777216 | tf_op jit(solution)/shard_map/pallas_call | solution.py:293
  97.2 0.0 copy-start
  97.3 0.0 copy-start.1
  97.3 3.7 %convert_reduce_fusion = f32[128,4096]{1,0:T(8,128)} fusion(bf16[2,128,4096]{2,1,0:T(8,128)(2,1)} %get-tuple-element.5), kind=kLoop, calls=%fused_computation | loop fusion | flops 1572864 | bytes 4194304 | tf_op jit(solution)/shard_map/reduce_sum | solution.py:326
  100.9 0.0 copy-done
  100.9 0.0 copy-done.1
  100.9 1.8 %fusion = f32[256,2048]{1,0:T(8,128)} fusion(f32[256,2048]{1,0:T(8,128)S(1)} %copy-done.1, bf16[2,256,2048]{2,1,0:T(8,128)(2,1)S(1)} %copy-done), kind=kLoop, calls=%fused_computation.2 | loop fusion | flops 2621440 | bytes 6291456 | tf_op jit(solution)/shard_map/div | solution.py:328
Async XLA Ops:
  97.2 3.7 %copy-start = (bf16[2,256,2048]{2,1,0:T(8,128)(2,1)S(1)}, bf16[2,256,2048]{2,1,0:T(8,128)(2,1)}, u32[]{:S(2)}) copy-start(bf16[2,256,2048]{2,1,0:T(8,128)(2,1)} %get-tuple-element.7) | copy-start | bytes 6291460
  97.3 3.7 %copy-start.1 = (f32[256,2048]{1,0:T(8,128)S(1)}, f32[256,2048]{1,0:T(8,128)}, u32[]{:S(2)}) copy-start(f32[256,2048]{1,0:T(8,128)} %get-tuple-element.6) | copy-start | bytes 6291460

commit v3 on v2

--- a/solution.py
+++ b/solution.py
@@ -104,6 +104,8 @@
     gcopy(1, 0, q, far).start()
     gcopy(0, 0, q, sib).start()
     send_acts_for(1)
+    gcopy(1, 1, q, far).start()
+    gcopy(0, 1, q, sib).start()
     own_go = pltpu.make_async_copy(go, go_l.at[part(q, rg)], l_sem.at[0])
     own_go.start()
     own_w = pltpu.make_async_copy(w, wall.at[part(z, blk)], l_sem.at[1])
@@ -112,16 +114,20 @@
     def gather_piece(s):
         gcopy(1, s, far, far).wait_recv()
 
-        @pl.when(s + 1 < PIECES)
-        def _():
-            gcopy(1, s + 1, q, far).start()
-            gcopy(0, s + 1, q, sib).start()
-
         gcopy(2, s, far, sib).start()
 
+        @pl.when(s + 2 < PIECES)
+        def _():
+            gcopy(1, s + 2, q, far).start()
+            gcopy(0, s + 2, q, sib).start()
+
+        @pl.when(s == PIECES - 2)
+        def _():
+            send_acts_for(2)
+
         @pl.when(s == PIECES - 1)
         def _():
-            for t in range(2, nz):
+            for t in range(3, nz):
                 send_acts_for(t)
             send_acts(z)
 
@@ -320,9 +326,9 @@
             pltpu.SemaphoreType.DMA((2,)),
         ],
         compiler_params=pltpu.CompilerParams(
-            collective_id=0, has_side_effects=True, vmem_limit_bytes=62 * 1024 * 1024),
+            collective_id=0, has_side_effects=True, vmem_limit_bytes=40 * 1024 * 1024),
         cost_estimate=pl.CostEstimate(flops=flops, bytes_accessed=16 * 1024 * 1024, transcendentals=0),
-    )(acts, grad_out, proj_weight)
+    )(*[pltpu.with_memory_space_constraint(a, pltpu.HBM) for a in (acts, grad_out, proj_weight)])
     grad_acts = jnp.sum(parts.astype(F32), axis=0)
     summed = own + sums[0].astype(F32) + sums[1].astype(F32)
     grad_weight = summed / jnp.sqrt(jnp.float32(total_tokens))

time: 104 us -> 102 us (0.981)
  other arithmetic: 5.42 us -> 3.51 us
    reduce_sum x1, other arithmetic: 3.65 us -> 1.7 us  [per_device(): grad_acts = jnp.sum(parts.astype(F32), axis=0)]
where the time goes in v3:
time: 102 us; the launch traced here: 100 us
  Pallas kernels  96.1 us (94%)
  other arithmetic  3.51 us (3%)
    pallas_call x1, Pallas kernels, per_device(): pl.pallas_call(functools.partial(kernel, nz, ns), out_shape=(jax.ShapeDty...  96.1 us

profile of v3, /device:TPU:17, one launch (start us, length us, event | category | flops | bytes accessed | tf_op | source)
XLA Modules:
  0.0 100.2 jit_solution(9196990453542999383)
XLA Ops:
  0.6 96.1 %shard_map.50 = (bf16[2,128,4096]{2,1,0:T(8,128)(2,1)S(1)}, bf16[2,256,2048]{2,1,0:T(8,128)(2,1)S(1)}, f32[256,2048]{1,0:T(8,128)S(1)}) custom-call(bf16[128,4096]{1,0:T(8,128)(2,1)} %acts.1, bf16[256,2048]{1,0:T(8,128)(2,1)} %go.1, bf16[256,2048]{1,0:T(8,128)(2,1)} %w.1), custom_call_target="tpu_custom_call" | custom-call | flops 8589934592 | bytes 16777216 | tf_op jit(solution)/shard_map/pallas_call | solution.py:299
  96.7 1.7 %convert_reduce_fusion = f32[128,4096]{1,0:T(8,128)} fusion(bf16[2,128,4096]{2,1,0:T(8,128)(2,1)S(1)} %get-tuple-element.5), kind=kLoop, calls=%fused_computation | loop fusion | flops 1572864 | bytes 4194304 | tf_op jit(solution)/shard_map/reduce_sum | solution.py:332
  98.4 1.8 %fusion = f32[256,2048]{1,0:T(8,128)} fusion(f32[256,2048]{1,0:T(8,128)S(1)} %get-tuple-element.6, bf16[2,256,2048]{2,1,0:T(8,128)(2,1)S(1)} %get-tuple-element.7), kind=kLoop, calls=%fused_computation.2 | loop fusion | flops 2621440 | bytes 6291456 | tf_op jit(solution)/shard_map/div | solution.py:334

commit v4 on v3

--- a/solution.py
+++ b/solution.py
@@ -62,7 +62,7 @@
     def wall_piece(i, s):
         return wall.at[pl.ds(pl.multiple_of(i * blk + s * h, h), h)]
 
-    for s in range(PIECES):
+    def send_weight(s):
         for d in range(2):
             @pl.when(pos[d] < nz - 1)
             def _():
@@ -103,7 +103,9 @@
 
     gcopy(1, 0, q, far).start()
     gcopy(0, 0, q, sib).start()
+    send_weight(0)
     send_acts_for(1)
+    send_weight(1)
     gcopy(1, 1, q, far).start()
     gcopy(0, 1, q, sib).start()
     own_go = pltpu.make_async_copy(go, go_l.at[part(q, rg)], l_sem.at[0])
@@ -120,6 +122,7 @@
         def _():
             gcopy(1, s + 2, q, far).start()
             gcopy(0, s + 2, q, sib).start()
+            send_weight(s + 2)
 
         @pl.when(s == PIECES - 2)
         def _():

time: 102 us -> 102 us (level)
  no operation moved by 1% of the time
where the time goes in v4:
time: 102 us; the launch traced here: 100 us
  Pallas kernels  96.1 us (94%)
  other arithmetic  3.51 us (3%)
    pallas_call x1, Pallas kernels, per_device(): pl.pallas_call(functools.partial(kernel, nz, ns), out_shape=(jax.ShapeDty...  96.1 us

profile of v4, /device:TPU:17, one launch (start us, length us, event | category | flops | bytes accessed | tf_op | source)
XLA Modules:
  0.0 100.2 jit_solution(9737865981717798269)
XLA Ops:
  0.6 96.1 %shard_map.50 = (bf16[2,128,4096]{2,1,0:T(8,128)(2,1)S(1)}, bf16[2,256,2048]{2,1,0:T(8,128)(2,1)S(1)}, f32[256,2048]{1,0:T(8,128)S(1)}) custom-call(bf16[128,4096]{1,0:T(8,128)(2,1)} %acts.1, bf16[256,2048]{1,0:T(8,128)(2,1)} %go.1, bf16[256,2048]{1,0:T(8,128)(2,1)} %w.1), custom_call_target="tpu_custom_call" | custom-call | flops 8589934592 | bytes 16777216 | tf_op jit(solution)/shard_map/pallas_call | solution.py:302
  96.7 1.7 %convert_reduce_fusion = f32[128,4096]{1,0:T(8,128)} fusion(bf16[2,128,4096]{2,1,0:T(8,128)(2,1)S(1)} %get-tuple-element.5), kind=kLoop, calls=%fused_computation | loop fusion | flops 1572864 | bytes 4194304 | tf_op jit(solution)/shard_map/reduce_sum | solution.py:335
  98.4 1.8 %fusion = f32[256,2048]{1,0:T(8,128)} fusion(f32[256,2048]{1,0:T(8,128)S(1)} %get-tuple-element.6, bf16[2,256,2048]{2,1,0:T(8,128)(2,1)S(1)} %get-tuple-element.7), kind=kLoop, calls=%fused_computation.2 | loop fusion | flops 2621440 | bytes 6291456 | tf_op jit(solution)/shard_map/div | solution.py:337

commit v5 on v4

--- a/solution.py
+++ b/solution.py
@@ -9,19 +9,18 @@
 
 MESH = pl.DeviceIdType.MESH
 NQ = 4
-PIECES = 4
 BF16 = jnp.bfloat16
 F32 = jnp.float32
 
 
-def kernel(nz, ns, acts, go, w, ga_out, rs_out, pz_out, go_l, acts_l, wall, ga_s,
+def kernel(nz, ns, pieces, acts, go, w, ga_out, rs_out, pz_out, go_l, acts_l, wall, ga_s,
            acts_t, rr, sb, pbuf, own, go_send, go_recv, a_send, a_recv, ga_send, ga_recv,
            z_send, z_recv, l_sem):
     tok = acts.shape[0]
     rg, cols = go.shape
     blk = w.shape[0]
-    h = blk // PIECES
-    pw = cols // PIECES
+    h = blk // pieces
+    pw = cols // pieces
     total = NQ * rg
     dp = lax.axis_index("dp")
     x = lax.axis_index("seq")
@@ -118,17 +117,17 @@
 
         gcopy(2, s, far, sib).start()
 
-        @pl.when(s + 2 < PIECES)
+        @pl.when(s + 2 < pieces)
         def _():
             gcopy(1, s + 2, q, far).start()
             gcopy(0, s + 2, q, sib).start()
             send_weight(s + 2)
 
-        @pl.when(s == PIECES - 2)
+        @pl.when(s == pieces - 2)
         def _():
             send_acts_for(2)
 
-        @pl.when(s == PIECES - 1)
+        @pl.when(s == pieces - 1)
         def _():
             for t in range(3, nz):
                 send_acts_for(t)
@@ -210,7 +209,7 @@
             zcopy(d, t, s, piece, piece).start()
 
     for t in range(1, nz):
-        @pl.loop(0, PIECES)
+        @pl.loop(0, pieces)
         def _(s):
             if t == 1:
                 gather_piece(s)
@@ -232,7 +231,7 @@
                     forward_sum(d, t, s)
 
             if t == 1:
-                @pl.when(s == PIECES - 1)
+                @pl.when(s == pieces - 1)
                 def _():
                     input_grad(z)
             else:
@@ -248,7 +247,7 @@
 
     turn_acts(z, 0)
 
-    @pl.loop(0, PIECES)
+    @pl.loop(0, pieces)
     def _(s):
         own[:, part(s, pw)] = weight_piece(0, s)
 
@@ -257,15 +256,15 @@
     for d in range(2):
         @pl.when(pos[d] == 0)
         def _():
-            rr[d, 0] = jnp.zeros((PIECES, blk, pw), BF16)
-            for s in range(PIECES):
+            rr[d, 0] = jnp.zeros((pieces, blk, pw), BF16)
+            for s in range(pieces):
                 fill = pltpu.make_async_copy(rr.at[d, 0, s], rs_out.at[d, :, part(s, pw)], l_sem.at[1])
                 fill.start()
                 fill.wait()
 
         @pl.when(pos[d] > 0)
         def _():
-            for s in range(PIECES):
+            for s in range(pieces):
                 piece = rs_out.at[d, :, part(s, pw)]
                 zcopy(d, nz - 1, s, piece, piece).wait_recv()
 
@@ -275,12 +274,12 @@
         @pl.when(pos[d] < nz - 1)
         def _():
             for t in range(nz):
-                @pl.loop(0, PIECES)
+                @pl.loop(0, pieces)
                 def _(s):
                     piece = sb.at[d, 0, s]
                     zcopy(d, t, s, piece, piece).wait_send()
     for k in range(3):
-        @pl.loop(0, PIECES)
+        @pl.loop(0, pieces)
         def _(s):
             gcopy(k, s, q, sib).wait_send()
     others = acts_l.at[pl.ds(0, total - tok)]
@@ -296,11 +295,12 @@
     rg, cols = grad_out.shape
     blk = proj_weight.shape[0]
     total_tokens = tok * ns * nz * NQ
+    pieces = min(8, cols // 128)
     total = NQ * rg
     anywhere = pl.BlockSpec(memory_space=pl.ANY)
     flops = 4 * total * nz * blk * cols
     parts, sums, own = pl.pallas_call(
-        functools.partial(kernel, nz, ns),
+        functools.partial(kernel, nz, ns, pieces),
         out_shape=(
             jax.ShapeDtypeStruct((ns, tok, feats), BF16),
             jax.ShapeDtypeStruct((2, blk, cols), BF16),
@@ -314,18 +314,18 @@
             pltpu.VMEM((nz * blk, cols), BF16),
             pltpu.VMEM((total, nz * blk), BF16),
             pltpu.VMEM((2, blk, total), BF16),
-            pltpu.VMEM((2, nz - 1, PIECES, blk, cols // PIECES), BF16),
-            pltpu.VMEM((2, nz - 1, PIECES, blk, cols // PIECES), BF16),
-            pltpu.VMEM((2, blk, cols // PIECES), F32),
+            pltpu.VMEM((2, nz - 1, pieces, blk, cols // pieces), BF16),
+            pltpu.VMEM((2, nz - 1, pieces, blk, cols // pieces), BF16),
+            pltpu.VMEM((2, blk, cols // pieces), F32),
             pltpu.VMEM((blk, cols), F32),
-            pltpu.SemaphoreType.DMA((3, PIECES)),
-            pltpu.SemaphoreType.DMA((3, PIECES)),
+            pltpu.SemaphoreType.DMA((3, pieces)),
+            pltpu.SemaphoreType.DMA((3, pieces)),
             pltpu.SemaphoreType.DMA,
             pltpu.SemaphoreType.DMA((nz,)),
             pltpu.SemaphoreType.DMA,
             pltpu.SemaphoreType.DMA,
-            pltpu.SemaphoreType.DMA((2, nz, PIECES)),
-            pltpu.SemaphoreType.DMA((2, nz, PIECES)),
+            pltpu.SemaphoreType.DMA((2, nz, pieces)),
+            pltpu.SemaphoreType.DMA((2, nz, pieces)),
             pltpu.SemaphoreType.DMA((2,)),
         ],
         compiler_params=pltpu.CompilerParams(

time: 102 us -> 103 us (level); the launches traced: 100 us -> 103 us
  Pallas kernels: 96.1 us -> 98.7 us
    pallas_call x1, Pallas kernels: 96.1 us -> 98.7 us  [per_device(): pl.pallas_call(functools.partial(kernel, nz, ns, pieces), out_shape=(jax....]
where the time goes in v5:
time: 103 us
  Pallas kernels  98.7 us (96%)
  other arithmetic  3.51 us (3%)
    pallas_call x1, Pallas kernels, per_device(): pl.pallas_call(functools.partial(kernel, nz, ns, pieces), out_shape=(jax....  98.7 us

profile of v5, /device:TPU:17, one launch (start us, length us, event | category | flops | bytes accessed | tf_op | source)
XLA Modules:
  0.0 102.9 jit_solution(11090889184447519978)
XLA Ops:
  0.6 98.7 %shard_map.50 = (bf16[2,128,4096]{2,1,0:T(8,128)(2,1)S(1)}, bf16[2,256,2048]{2,1,0:T(8,128)(2,1)S(1)}, f32[256,2048]{1,0:T(8,128)S(1)}) custom-call(bf16[128,4096]{1,0:T(8,128)(2,1)} %acts.1, bf16[256,2048]{1,0:T(8,128)(2,1)} %go.1, bf16[256,2048]{1,0:T(8,128)(2,1)} %w.1), custom_call_target="tpu_custom_call" | custom-call | flops 8589934592 | bytes 16777216 | tf_op jit(solution)/shard_map/pallas_call | solution.py:302
  99.4 1.7 %convert_reduce_fusion = f32[128,4096]{1,0:T(8,128)} fusion(bf16[2,128,4096]{2,1,0:T(8,128)(2,1)S(1)} %get-tuple-element.5), kind=kLoop, calls=%fused_computation | loop fusion | flops 1572864 | bytes 4194304 | tf_op jit(solution)/shard_map/reduce_sum | solution.py:335
  101.1 1.8 %fusion = f32[256,2048]{1,0:T(8,128)} fusion(f32[256,2048]{1,0:T(8,128)S(1)} %get-tuple-element.6, bf16[2,256,2048]{2,1,0:T(8,128)(2,1)S(1)} %get-tuple-element.7), kind=kLoop, calls=%fused_computation.2 | loop fusion | flops 2621440 | bytes 6291456 | tf_op jit(solution)/shard_map/div | solution.py:337

commit v6 on v5

--- a/solution.py
+++ b/solution.py
@@ -295,7 +295,7 @@
     rg, cols = grad_out.shape
     blk = proj_weight.shape[0]
     total_tokens = tok * ns * nz * NQ
-    pieces = min(8, cols // 128)
+    pieces = min(2, cols // 128)
     total = NQ * rg
     anywhere = pl.BlockSpec(memory_space=pl.ANY)
     flops = 4 * total * nz * blk * cols

time: 103 us -> 102 us (level)
  Pallas kernels: 98.7 us -> 97.3 us
    pallas_call x1, Pallas kernels: 98.7 us -> 97.3 us  [per_device(): pl.pallas_call(functools.partial(kernel, nz, ns, pieces), out_shape=(jax....]
where the time goes in v6:
time: 102 us
  Pallas kernels  97.3 us (95%)
  other arithmetic  3.51 us (3%)
    pallas_call x1, Pallas kernels, per_device(): pl.pallas_call(functools.partial(kernel, nz, ns, pieces), out_shape=(jax....  97.3 us

profile of v6, /device:TPU:17, one launch (start us, length us, event | category | flops | bytes accessed | tf_op | source)
XLA Modules:
  0.0 101.5 jit_solution(8461617998332807176)
XLA Ops:
  0.6 97.3 %shard_map.50 = (bf16[2,128,4096]{2,1,0:T(8,128)(2,1)S(1)}, bf16[2,256,2048]{2,1,0:T(8,128)(2,1)S(1)}, f32[256,2048]{1,0:T(8,128)S(1)}) custom-call(bf16[128,4096]{1,0:T(8,128)(2,1)} %acts.1, bf16[256,2048]{1,0:T(8,128)(2,1)} %go.1, bf16[256,2048]{1,0:T(8,128)(2,1)} %w.1), custom_call_target="tpu_custom_call" | custom-call | flops 8589934592 | bytes 16777216 | tf_op jit(solution)/shard_map/pallas_call | solution.py:302
  98.0 1.7 %convert_reduce_fusion = f32[128,4096]{1,0:T(8,128)} fusion(bf16[2,128,4096]{2,1,0:T(8,128)(2,1)S(1)} %get-tuple-element.5), kind=kLoop, calls=%fused_computation | loop fusion | flops 1572864 | bytes 4194304 | tf_op jit(solution)/shard_map/reduce_sum | solution.py:335
  99.7 1.8 %fusion = f32[256,2048]{1,0:T(8,128)} fusion(f32[256,2048]{1,0:T(8,128)S(1)} %get-tuple-element.6, bf16[2,256,2048]{2,1,0:T(8,128)(2,1)S(1)} %get-tuple-element.7), kind=kLoop, calls=%fused_computation.2 | loop fusion | flops 2621440 | bytes 6291456 | tf_op jit(solution)/shard_map/div | solution.py:337

commit v7 on v6

--- a/solution.py
+++ b/solution.py
@@ -2,6 +2,7 @@
 
 import jax
 import jax.numpy as jnp
+import numpy as np
 from jax import lax
 from jax.experimental import pallas as pl
 from jax.experimental.pallas import tpu as pltpu
@@ -286,6 +287,27 @@
     pltpu.make_async_copy(others, others, a_send).wait()
     others = ga_s.at[pl.ds(0, total - tok)]
     pltpu.make_async_copy(others, others, ga_send).wait()
+
+
+def finish(ns, root, parts, sums, own, ga, gw, ga_buf, gw_buf, sem):
+    def emit(out, buf, k, step, value):
+        @pl.loop(0, buf.shape[0] // step)
+        def _(i):
+            r = pl.ds(pl.multiple_of(i * step, step), step)
+            buf[r, :] = value(r)
+            pltpu.make_async_copy(buf.at[r], out.at[r], sem.at[k]).start()
+
+    def added(r):
+        value = parts[0, r, :].astype(F32)
+        for j in range(1, ns):
+            value = value + parts[j, r, :].astype(F32)
+        return value
+
+    emit(ga, ga_buf, 0, 16, added)
+    emit(gw, gw_buf, 1, 32,
+         lambda r: (own[r, :] + sums[0, r, :].astype(F32) + sums[1, r, :].astype(F32)) / root)
+    pltpu.make_async_copy(ga_buf, ga, sem.at[0]).wait()
+    pltpu.make_async_copy(gw_buf, gw, sem.at[1]).wait()
 
 
 def per_device(acts, grad_out, proj_weight):
@@ -332,10 +354,16 @@
             collective_id=0, has_side_effects=True, vmem_limit_bytes=40 * 1024 * 1024),
         cost_estimate=pl.CostEstimate(flops=flops, bytes_accessed=16 * 1024 * 1024, transcendentals=0),
     )(*[pltpu.with_memory_space_constraint(a, pltpu.HBM) for a in (acts, grad_out, proj_weight)])
-    grad_acts = jnp.sum(parts.astype(F32), axis=0)
-    summed = own + sums[0].astype(F32) + sums[1].astype(F32)
-    grad_weight = summed / jnp.sqrt(jnp.float32(total_tokens))
-    return (grad_acts, grad_weight)
+    root = np.sqrt(np.float32(total_tokens))
+    shapes = ((tok, feats), (blk, cols))
+    return pl.pallas_call(
+        functools.partial(finish, ns, root),
+        out_shape=tuple(jax.ShapeDtypeStruct(shape, F32) for shape in shapes),
+        in_specs=[pl.BlockSpec(memory_space=pltpu.VMEM)] * 3,
+        out_specs=(anywhere,) * 2,
+        scratch_shapes=[pltpu.VMEM(shape, F32) for shape in shapes] + [pltpu.SemaphoreType.DMA((2,))],
+        compiler_params=pltpu.CompilerParams(vmem_limit_bytes=40 * 1024 * 1024),
+    )(parts, sums, own)
 
 
 def solution(mesh):

time: 102 us -> 100 us (0.980)
  other arithmetic: 3.51 us -> 0 us
  Pallas kernels: 97.3 us -> 99.4 us
    pallas_call x0 -> x1, Pallas kernels: none -> 2.04 us  [per_device(): pl.pallas_call(functools.partial(finish, ns, root), out_shape=tuple((jax....]
    div x1 -> x0, other arithmetic: 1.81 us -> none  [per_device(): grad_weight = summed / jnp.sqrt(jnp.float32(total_tokens))]
    reduce_sum x1 -> x0, other arithmetic: 1.7 us -> none  [per_device(): grad_acts = jnp.sum(parts.astype(F32), axis=0)]
where the time goes in v7:
time: 100 us
  Pallas kernels  99.4 us (99%)
    pallas_call x1, Pallas kernels, per_device(): pl.pallas_call(functools.partial(kernel, nz, ns, pieces), out_shape=(jax....  97.3 us
    pallas_call x1, Pallas kernels, per_device(): pl.pallas_call(functools.partial(finish, ns, root), out_shape=tuple((jax....  2.04 us

profile of v7, /device:TPU:17, one launch (start us, length us, event | category | flops | bytes accessed | tf_op | source)
XLA Modules:
  0.0 100.0 jit_solution(15867821824152791575)
XLA Ops:
  0.6 97.3 %shard_map.50 = (bf16[2,128,4096]{2,1,0:T(8,128)(2,1)S(1)}, bf16[2,256,2048]{2,1,0:T(8,128)(2,1)S(1)}, f32[256,2048]{1,0:T(8,128)S(1)}) custom-call(bf16[128,4096]{1,0:T(8,128)(2,1)} %acts.1, bf16[256,2048]{1,0:T(8,128)(2,1)} %go.1, bf16[256,2048]{1,0:T(8,128)(2,1)} %w.1), custom_call_target="tpu_custom_call" | custom-call | flops 8589934592 | bytes 16777216 | tf_op jit(solution)/shard_map/pallas_call | solution.py:324
  98.0 2.0 %shard_map.51 = (f32[128,4096]{1,0:T(8,128)}, f32[256,2048]{1,0:T(8,128)}) custom-call(bf16[2,128,4096]{2,1,0:T(8,128)(2,1)S(1)} %get-tuple-element.5.parts, bf16[2,256,2048]{2,1,0:T(8,128)(2,1)S(1)} %get-tuple-element.6.sums, f32[256,2048]{1,0:T(8,128)S(1)} %get-tuple-element.7.own), custom_call_target="tpu_custom_call" | custom-call | tf_op jit(solution)/shard_map/pallas_call | solution.py:359
